TPU v7x, 32 devices: a whole 2x2x4 slice. The times are simulated.
32 devices in a mesh: pack: 8 (over z, y), hist: 4 (over x, core).
Axes of the slice: x: 2, y: 2, z: 4, core: 2. Of those that a mesh axis runs over, the one named last changes fastest.
Arguments:
- queries: bfloat16 [8, 2048, 2048], P('pack', 'hist'), may hold values from -0.59765625 to 0.59765625
- keys: bfloat16 [8, 2048, 2048], P('pack', 'hist'), may hold values from -6 to 6
- values: bfloat16 [8, 2048, 2048], P('pack', 'hist'), may hold values from -6 to 6
- gates: bfloat16 [8, 2048, 2048], P('pack', 'hist'), may hold values from -6 to 6
- user_ids: int32 [8, 2048], P('pack', 'hist'), may hold values from 0 to 5, never falling along the last dimension, each value on 1 to 682 neighbouring positions
- forget_rate: float32 [16], replicated, may hold values from 0.0001 to 0.02
- norm_gain: float32 [2048], replicated, may hold values from 0.1 to 1.9
- w_out: bfloat16 [2048, 2048], P('pack'), may hold values from -0.125 to 0.125
Outputs:
- mixed: bfloat16 [8, 2048, 2048], P('pack', 'hist')
Inputs may be any that keep to these rules, and one draw needn't show every extreme that they name: `user_ids`: in each window user ids never fall along the events; each user holds 1 to 682 consecutive events, and one user exactly 682.
All inputs are finite; a program needn't handle non-finite values.
Results may differ from a plain program's by a relative error of at most 0.0061.
Values may be sent and summed in bfloat16 or wider, within the bound.
A program may use at most 128 MiB of HBM per device.

v0:
```python
import jax
import jax.numpy as jnp
from jax import lax
from jax.sharding import PartitionSpec as P

HEADS = 16
GROUP = 128


def passed_along(array, axis, by):
    size = lax.axis_size(axis)
    pairs = [(i, i + by) for i in range(size) if 0 <= i + by < size]
    return lax.ppermute(array, axis, pairs)


def carried_in(array, axis, combine, identity):
    size, here = (lax.axis_size(axis), lax.axis_index(axis))
    everything = jax.tree.map(lambda part: lax.all_gather(part, axis), array)
    start = jax.tree.map(
        lambda part, zero: jnp.broadcast_to(jnp.asarray(zero, part.dtype), part.shape),
        array,
        identity,
    )

    def hop(k, before):
        reached = k < here
        new = combine(before, jax.tree.map(lambda part: part[k], everything))
        return jax.tree.map(lambda a, b: jnp.where(reached, a, b), new, before)

    return lax.fori_loop(0, size, hop, start)


def combine_states(earlier, later):
    return (earlier[0] * later[0], later[0][:, None, None] * earlier[1] + later[1])


def local(queries, keys, values, gates, user_ids, forget_rate, norm_gain, w_out):
    length = queries.shape[1]
    width = queries.shape[2]
    head_dim = width // HEADS
    blocks = length // GROUP
    log_decay = jnp.log1p(-forget_rate)
    users = user_ids[0]
    before = passed_along(users[length - 1 :], "hist", 1)
    prior = jnp.concatenate([before, users[:-1]])
    place_all = jnp.arange(length, dtype=jnp.int32)
    forced = jnp.logical_and(lax.axis_index("hist") == 0, place_all == 0)
    starts = jnp.logical_or(users != prior, forced).astype(jnp.int32)
    seg = users.reshape(blocks, GROUP)
    start_blk = starts.reshape(blocks, GROUP)
    q_blk = queries[0].reshape(blocks, GROUP, HEADS, head_dim)
    k_blk = keys[0].reshape(blocks, GROUP, HEADS, head_dim)
    v_blk = values[0].reshape(blocks, GROUP, HEADS, head_dim)
    place = jnp.arange(GROUP, dtype=jnp.int32)
    diff = place[:, None] - place[None, :]
    causal = diff >= 0
    lag = jnp.where(causal, diff, 0).astype(jnp.float32)
    decay = jnp.exp(lag[None] * log_decay[:, None, None])
    mask = jnp.logical_and(seg[:, :, None] == seg[:, None, :], causal[None])
    scores = jnp.einsum("nthd,nshd->nhts", q_blk, k_blk, preferred_element_type=jnp.float32)
    weights = jnp.where(mask[:, None], scores * decay[None], 0.0).astype(jnp.bfloat16)
    inner = jnp.einsum("nhts,nshd->nthd", weights, v_blk, preferred_element_type=jnp.float32)
    tail = jnp.exp((GROUP - 1 - place).astype(jnp.float32)[None, :] * log_decay[:, None])
    keep_rows = (seg == seg[:, -1:]).astype(jnp.float32)
    scaled = (k_blk * (keep_rows[:, :, None] * tail.T[None])[..., None]).astype(jnp.bfloat16)
    own = jnp.einsum("nshd,nshe->nhde", scaled, v_blk, preferred_element_type=jnp.float32)
    any_start = jnp.max(start_blk, axis=1) > 0
    keep = jnp.where(any_start[:, None], 0.0, jnp.exp(GROUP * log_decay)[None, :])

    def advance(state, item):
        keep_c, own_c = item
        return (keep_c[:, None, None] * state + own_c, state)

    zero_state = jnp.zeros((HEADS, head_dim, head_dim), jnp.float32)
    local_final, local_enter = lax.scan(advance, zero_state, (keep, own))
    keep_before = jnp.cumprod(
        jnp.concatenate([jnp.ones((1, HEADS), jnp.float32), keep[:-1]], axis=0), axis=0
    )
    keep_device = keep_before[-1] * keep[-1]
    identity = (
        jnp.ones((HEADS,), jnp.float32),
        jnp.zeros((HEADS, head_dim, head_dim), jnp.float32),
    )
    incoming = carried_in((keep_device, local_final), "hist", combine_states, identity)[1]
    entering = (local_enter + keep_before[:, :, None, None] * incoming[None]).astype(jnp.bfloat16)
    open_run = (jnp.cumsum(start_blk, axis=1) == 0).astype(jnp.float32)
    reach = jnp.exp((place + 1).astype(jnp.float32)[:, None] * log_decay[None, :])
    factor = open_run[:, :, None] * reach[None]
    carried = (
        jnp.einsum("nthd,nhde->nthe", q_blk, entering, preferred_element_type=jnp.float32)
        * factor[..., None]
    )
    retained = (inner + carried).reshape(length, HEADS, head_dim)
    mean = jnp.mean(retained, axis=2, keepdims=True)
    centred = retained - mean
    variance = jnp.mean(centred * centred, axis=2, keepdims=True)
    normed = (centred * lax.rsqrt(variance + 1e-05)).reshape(length, width) * norm_gain
    gated = (jax.nn.silu(gates[0].astype(jnp.float32)) * normed).astype(jnp.bfloat16)
    mixed = jnp.dot(
        gated, lax.all_gather(w_out, "pack", axis=0, tiled=True), preferred_element_type=jnp.float32
    ).astype(jnp.bfloat16)
    return mixed[None]


def solution(mesh):
    in_specs = (
        P("pack", "hist", None),
        P("pack", "hist", None),
        P("pack", "hist", None),
        P("pack", "hist", None),
        P("pack", "hist"),
        P(),
        P(),
        P("pack", None),
    )
    out_specs = P("pack", "hist", None)
    return jax.shard_map(local, mesh=mesh, in_specs=in_specs, out_specs=out_specs, check_vma=False)
```

profile of v0, /device:TPU:0, one launch (start us, length us, event | category | flops | bytes accessed | tf_op | source)
XLA Modules:
  0.0 226.9 jit_solution(9160905104936268966)
XLA Ops:
  6.5 1.3 slice.26
  7.8 2.8 %collective-permute-start = (s32[1]{0:T(128)}, s32[1]{0:T(128)}, u32[]{:S(2)}, u32[]{:S(2)}) collective-permute-start(s32[1]{0:T(128)} %bitcast.4), channel_id=1, source_target_pairs={{0,1},{1,2},{2,3},{4,5},{5,6},{6,7},{8,9},{9,10},{10,11},{12,13},{... | collective-permute-start | bytes 20 | tf_op jit(solution)/shard_map/ppermute | solution.py:13
  10.7 0.9 slice_reduce_fusion
  11.6 0.8 compare_convert_fusion.1
  12.3 0.7 multiply_exponential_fusion.3
  13.0 3.5 %copy.41 = bf16[64,8,16,128]{3,2,1,0:T(8,128)(2,1)} copy(bf16[64,8,16,128]{3,1,2,0:T(8,128)(2,1)} %bitcast.105) | data formatting | bytes 4194304
  16.5 3.5 %copy.26 = bf16[4,128,16,128]{1,3,2,0:T(8,128)(2,1)S(1)} copy(bf16[4,128,16,128]{3,2,1,0:T(8,128)(2,1)} %bitcast.100) | data formatting | bytes 4194304 | tf_op jit(solution)/shard_map/reshape;squeeze | solution.py:52
  20.0 4.3 %copy.42 = bf16[64,8,16,128]{3,2,1,0:T(8,128)(2,1)} copy(bf16[64,8,16,128]{3,1,2,0:T(8,128)(2,1)} %bitcast.106) | data formatting | bytes 4194304
  24.3 0.1 multiply_exponential_fusion.1
  24.4 0.0 collective-permute-done
  24.4 0.8 fusion.31
  25.2 0.3 reduce_window_sum.11
  25.5 0.1 broadcast_select_fusion
  25.6 4.3 %fusion.10 = f32[4,16,128,128]{3,2,1,0:T(8,128)} fusion(bf16[4,128,16,128]{1,3,2,0:T(8,128)(2,1)S(1)} %copy.26, f32[4,128,16]{1,2,0:T(8,128)S(1)} %get-tuple-element.195, bf16[4,128,16,128]{3,2,1,0:T(8,128)(2,1)} %bitcast.98), kind=kOutput, calls=%fused_computation.25 | convolution fusion | flops 271581184 | bytes 8421376 | tf_op jit(solution)/shard_map/nshd,nshe->nhde/dot_general | solution.py:66
  29.9 10.0 %while.29 = (s32[]{:T(128)}, f32[16,128,128]{2,1,0:T(8,128)S(1)}, f32[4,16,128,128]{3,2,1,0:T(8,128)}, f32[4,16]{1,0:T(4,128)S(1)}, f32[4,16,128,128]{3,2,1,0:T(8,128)}) while((s32[]{:T(128)}, f32[16,128,128]{2,1,0:T(8,128)S(1)}, f32[4,16,128,128]{3,2,1,0:T(8,128)}, f32[4,16]{1,0:T(4,128)S(1)}, ...), condition=%wide.region_2.3_spmd.clone.clone, body=%wide.region_1.2_spmd.clone.sunk.clone | while | flops 1048579 | bytes 5243664 | solution.py:75
  29.9 1.1 bitcast_dynamic-update-slice_fusion.3
  30.9 1.4 bitcast_add_fusion.4
  32.4 1.1 bitcast_dynamic-update-slice_fusion.3
  33.5 1.4 bitcast_add_fusion.4
  34.9 1.1 bitcast_dynamic-update-slice_fusion.3
  36.0 1.4 bitcast_add_fusion.4
  37.4 1.1 bitcast_dynamic-update-slice_fusion.3
  38.5 1.4 bitcast_add_fusion.4
  39.9 1.0 copy-done
  40.9 0.0 all-gather.7.cloned.1.call-update
  41.0 0.0 all-gather.5.cloned.1.call-start
  41.0 0.7 all-gather.5.cloned.1.call-update
  41.7 2.2 copy.40
  44.0 0.1 compare_and_fusion
  44.1 1.2 multiply_exponential_fusion
  45.3 7.0 %fusion.17 = f32[4,16,128,128]{2,3,1,0:T(8,128)} fusion(bf16[4,128,16,128]{3,2,1,0:T(8,128)(2,1)} %bitcast.99, bf16[4,128,16,128]{1,3,2,0:T(8,128)(2,1)} %copy-done.1, f32[16,128,128]{2,1,0:T(8,128)} %multiply_exponential_fusion, pred[4,128,128]{2,1,0:T(8,128)(4,1)S(1)} %compare_and_fusion, bf16[4,128,16,128]{3,2,1,0:T(8,128)(2,1)S(1)} %bitcast.96), kind=kOutput, calls=%fused_computation.31 | convolution fusion | flops 540016640 | bytes 11599872 | tf_op jit(solution)/shard_map/nhts,nshd->nthd/dot_general | solution.py:62
  52.3 6.5 %all-gather.1 = f32[4,1,16]{2,1,0:T(1,128)S(1)} all-gather(f32[1,1,16]{2,1,0:T(1,128)S(1)} %multiply_bitcast_fusion), channel_id=1, replica_groups=mesh['pack'=8,'hist'=4] {'hist'}, dimensions={0}, use_global_device_ids=true | all-gather | bytes 320 | tf_op jit(solution)/shard_map/all_gather | solution.py:18
  58.8 18.9 %all-gather.7.cloned.1.call-done = f32[64,128,128]{2,1,0:T(8,128)} async-done(((f32[16,128,128]{2,1,0:T(8,128)}), f32[64,128,128]{2,1,0:T(8,128)}) %all-gather.7.cloned.1.call-update) | async-done | bytes 4194320 | tf_op jit(solution)/shard_map/all_gather | solution.py:18
  77.7 6.0 %while.30 = (s32[]{:T(128)}, f32[16,128,128]{2,1,0:T(8,128)S(1)}, s32[]{:T(128)}, f32[4,16]{1,0:T(4,128)S(1)}, f32[4,16,128,128]{3,2,1,0:T(8,128)}) while((s32[]{:T(128)}, f32[16,128,128]{2,1,0:T(8,128)S(1)}, s32[]{:T(128)}, f32[4,16]{1,0:T(4,128)S(1)}, f32[4,16,128,128]{3,2,1,0:T(8,128)}) %tuple.71), condition=%wide.region_5.6_spmd.clone.clone, body=%wide.region_4.5_spmd.clone.sunk.clone | while | flops 1048580 | bytes 3146009 | solution.py:30
  77.7 1.5 fusion.41
  79.2 1.5 fusion.41
  80.7 1.5 fusion.41
  82.2 1.5 fusion.41
  83.7 7.4 %fusion.33 = (f32[4,128,16]{1,2,0:T(8,128)S(1)}, f32[4,128,16,128]{1,3,2,0:T(8,128)}) fusion(f32[4,128,16]{1,2,0:T(8,128)S(1)} %get-tuple-element.194, bf16[4,128,16,128]{3,2,1,0:T(8,128)(2,1)S(1)} %bitcast.97, f32[4,16,128,128]{3,2,1,0:T(8,128)} %get-tuple-element.127, f32[16,128,128]{2,1,0:T(8,128)S(1)} %get-tuple-element.129, ...), kind=kOutput, calls=%fused_computation.66 | convolution fusion | flops 274718720 | bytes 15794432 | tf_op jit(solution)/shard_map/nthd,nhde->nthe/dot_general | solution.py:90
  91.1 0.1 copy.36
  91.2 5.4 %copy.30 = f32[4,128,16,128]{3,2,1,0:T(8,128)} copy(f32[4,128,16,128]{1,3,2,0:T(8,128)} %get-tuple-element.193) | data formatting | bytes 8388608 | tf_op jit(solution)/shard_map/add | solution.py:93
  96.7 3.0 %multiply_reduce_fusion = f32[4,128,16]{1,2,0:T(8,128)S(1)} fusion(f32[4,128,16,128]{1,3,2,0:T(8,128)} %get-tuple-element.193, f32[4,128,16]{1,2,0:T(8,128)S(1)} %broadcast_multiply_fusion), kind=kLoop, calls=%fused_computation.18 | loop fusion | flops 3137536 | bytes 4259840 | tf_op jit(solution)/shard_map/reduce_sum | solution.py:96
  99.7 0.1 copy.37
  99.8 105.0 %all-gather.5.cloned.1.call-done = bf16[2048,2048]{1,0:T(8,128)(2,1)} async-done(((bf16[256,2048]{1,0:T(8,128)(2,1)}), bf16[2048,2048]{1,0:T(8,128)(2,1)}) %all-gather.5.cloned.1.call-update) | async-done | bytes 8388624 | tf_op jit(solution)/shard_map/all_gather | solution.py:100
  204.8 1.1 mul.221
  206.0 1.1 sub.57
  207.1 0.6 copy-done.4
  207.7 12.4 %fusion.9 = bf16[1,512,2048]{2,1,0:T(8,128)(2,1)} fusion(bf16[2048,2048]{1,0:T(8,128)(2,1)} %all-gather.5.cloned.1.call-done, f32[64,8,16,128]{3,2,1,0:T(8,128)S(1)} %bitcast.103, f32[64,8,16,128]{3,2,1,0:T(8,128)S(1)} %bitcast.104, f32[64,8,16,128]{3,2,1,0:T(8,128)S(1)} %bitcast.102, bf16[1,512,2048]{2,1,0:T(8,128)(2,1)S(1)} %copy-done.4, ...), kind=kOutput, calls=%fused_computation.24 | convolution fusion | flops 4306501632 | bytes 25174016 | tf_op jit(solution)/shard_map/dot_general | solution.py:99
  (33 shorter events, 0.2 us)
Async XLA Ops:
  6.5 71.2 %all-gather.7.cloned.1.call-start = ((), (), s32[]{:S(2)}) async-start(), calls=%async_computation.1 | async-start | bytes 5242880 | tf_op jit(solution)/shard_map/all_gather | solution.py:18
  7.8 16.5 %collective-permute-start = (s32[1]{0:T(128)}, s32[1]{0:T(128)}, u32[]{:S(2)}, u32[]{:S(2)}) collective-permute-start(s32[1]{0:T(128)} %bitcast.4), channel_id=1, source_target_pairs={{0,1},{1,2},{2,3},{4,5},{5,6},{6,7},{8,9},{9,10},{10,11},{12,13},{... | collective-permute-start | bytes 20 | tf_op jit(solution)/shard_map/ppermute | solution.py:13
  16.5 7.9 %copy-start.3 = (s32[1,512]{1,0:T(1,128)S(1)}, s32[1,512]{1,0:T(1,128)}, u32[]{:S(2)}) copy-start(s32[1,512]{1,0:T(1,128)} %param.16) | copy-start | bytes 6148
  20.0 9.9 %copy-start.1 = (bf16[4,128,16,128]{1,3,2,0:T(8,128)(2,1)}, bf16[4,128,16,128]{1,3,2,0:T(8,128)(2,1)S(1)}, u32[]{:S(2)}) copy-start(bf16[4,128,16,128]{1,3,2,0:T(8,128)(2,1)S(1)} %copy.26) | copy-start | bytes 6291460
  39.9 1.0 copy-start
  41.0 163.9 %all-gather.5.cloned.1.call-start = ((), (), s32[]{:S(2)}) async-start(), calls=%async_computation | async-start | bytes 9437184 | tf_op jit(solution)/shard_map/all_gather | solution.py:100
  204.8 2.3 %copy-start.2 = (f32[4,128,16,128]{3,2,1,0:T(8,128)S(1)}, f32[4,128,16,128]{3,2,1,0:T(8,128)}, u32[]{:S(2)}) copy-start(f32[4,128,16,128]{3,2,1,0:T(8,128)} %copy.30) | copy-start | bytes 12582916
  204.8 2.9 %copy-start.4 = (bf16[1,512,2048]{2,1,0:T(8,128)(2,1)S(1)}, bf16[1,512,2048]{2,1,0:T(8,128)(2,1)}, u32[]{:S(2)}) copy-start(bf16[1,512,2048]{2,1,0:T(8,128)(2,1)} %param.15) | copy-start | bytes 6291460
  204.8 2.9 %copy-start.5 = (f32[2048]{0:T(1024)S(1)}, f32[2048]{0:T(1024)}, u32[]{:S(2)}) copy-start(f32[2048]{0:T(1024)} %param.18) | copy-start | bytes 24580
Sparse Core Ops, SparseCore 0:
  41.1 36.6 all-gather.6
  79.9 124.9 all-gather.4
where the time goes:
time: 228 us; the launch traced here: 227 us
  waiting for transfers between devices  125 us (55%)
  matrix products  31.1 us (14%)
  local copies, waits for them, and re-layouts  25.3 us (11%)
  other arithmetic  22.9 us (10%)
  between operations  13.5 us (6%)
  blocking collectives  6.46 us (3%)
  starting transfers between devices  2.89 us (1%)
    all_gather x1, waiting for transfers between devices, local(): lax.all_gather(w_out, 'pack', axis=0, tiled=True)  105 us
    all_gather x1, waiting for transfers between devices, carried_in(): everything = jax.tree.map(lambda part: lax.all_gather(part, axis), array)  18.9 us
    dot_general x1, matrix products, local(): jnp.dot(gated, lax.all_gather(w_out, 'pack', axis=0, tiled=True), preferr...  12.4 us
    unnamed x15, local copies, waits for them, and re-layouts  11.6 us
    dot_general x1, matrix products, local(): jnp.einsum('nthd,nhde->nthe', q_blk, entering, preferred_element_type=jnp...  7.39 us
    dot_general x1, matrix products, local(): jnp.einsum('nhts,nshd->nthd', weights, v_blk, preferred_element_type=jnp....  6.97 us
    all_gather x1, blocking collectives, carried_in(): everything = jax.tree.map(lambda part: lax.all_gather(part, axis), array)  6.46 us
    select_n x4, other arithmetic, hop(): return jax.tree.map(lambda a, b: jnp.where(reached, a, b), new, before)  5.83 us
  transfers between devices with their start and end apart: 3, of which 2 were waited for; matrix products, arithmetic and copies ran while one was open for 20% of the time, Pallas kernels for 0%

commit v1 on v0

--- a/solution.py
+++ b/solution.py
@@ -1,6 +1,10 @@
+import functools
+
 import jax
 import jax.numpy as jnp
 from jax import lax
+from jax.experimental import pallas as pl
+from jax.experimental.pallas import tpu as pltpu
 from jax.sharding import PartitionSpec as P
 
 HEADS = 16
@@ -34,7 +38,7 @@
     return (earlier[0] * later[0], later[0][:, None, None] * earlier[1] + later[1])
 
 
-def local(queries, keys, values, gates, user_ids, forget_rate, norm_gain, w_out):
+def local_any(queries, keys, values, gates, user_ids, forget_rate, norm_gain, w_out):
     length = queries.shape[1]
     width = queries.shape[2]
     head_dim = width // HEADS
@@ -73,9 +77,10 @@
 
     zero_state = jnp.zeros((HEADS, head_dim, head_dim), jnp.float32)
     local_final, local_enter = lax.scan(advance, zero_state, (keep, own))
-    keep_before = jnp.cumprod(
-        jnp.concatenate([jnp.ones((1, HEADS), jnp.float32), keep[:-1]], axis=0), axis=0
-    )
+    products = [jnp.ones((HEADS,), jnp.float32)]
+    for c in range(blocks - 1):
+        products.append(products[-1] * keep[c])
+    keep_before = jnp.stack(products)
     keep_device = keep_before[-1] * keep[-1]
     identity = (
         jnp.ones((HEADS,), jnp.float32),
@@ -83,7 +88,9 @@
     )
     incoming = carried_in((keep_device, local_final), "hist", combine_states, identity)[1]
     entering = (local_enter + keep_before[:, :, None, None] * incoming[None]).astype(jnp.bfloat16)
-    open_run = (jnp.cumsum(start_blk, axis=1) == 0).astype(jnp.float32)
+    ahead = prior.reshape(blocks, GROUP)[:, :1]
+    first = starts.reshape(blocks, GROUP)[:, :1]
+    open_run = jnp.logical_and(seg == ahead, first == 0).astype(jnp.float32)
     reach = jnp.exp((place + 1).astype(jnp.float32)[:, None] * log_decay[None, :])
     factor = open_run[:, :, None] * reach[None]
     carried = (
@@ -102,6 +109,351 @@
     return mixed[None]
 
 
+HEAD_DIM = 128
+MESH = pl.DeviceIdType.MESH
+F32 = jnp.float32
+BF16 = jnp.bfloat16
+PARTS = 4
+Z_AT, Y_AT, X_AT, C_AT, COPIES = 0, 3, 7, 13, 26
+
+
+def fits(mesh):
+    return mesh.shape["pack"] == 8 and mesh.shape["hist"] == 4
+
+
+def fused(
+    rate_ref, q_hbm, k_hbm, v_hbm, g_hbm, users_ref, gain_ref, w_hbm, o_hbm,
+    q, k, v, g, w, gated, acc, out, local, final, s_in, s_out, prior, same, rows_last, opened,
+    load_sem, send_sem, recv_sem, state_send, state_recv, user_sem,
+):
+    length, width = q.shape
+    depth = w.shape[1]
+    quarter, half = depth // 4, depth // 2
+    blocks = length // GROUP
+    pack, hist = lax.axis_index("pack"), lax.axis_index("hist")
+    z, y = pack // 2, lax.rem(pack, 2)
+    x, core = hist // 2, lax.rem(hist, 2)
+    last_hist = 3
+
+    def pack_of(dz, dy):
+        return lax.rem(z + dz + 4, 4) * 2 + (y if dy == 0 else 1 - y)
+
+    y_peer = (pack_of(0, 1), hist)
+    x_peer = (pack, (1 - x) * 2 + core)
+    c_peer = (pack, x * 2 + 1 - core)
+    z_peers = [(pack_of(d, 0), hist) for d in range(1, 4)]
+
+    loads = []
+    for i, (src, dst) in enumerate([(k_hbm, k), (v_hbm, v), (q_hbm, q), (g_hbm, g), (w_hbm, w.at[pack])]):
+        loads.append(pltpu.make_async_copy(src, dst, load_sem.at[i]))
+        loads[-1].start()
+
+    barrier = pltpu.get_barrier_semaphore()
+    others = [(pack, lax.rem(hist + d, 4)) for d in range(1, 4)]
+    for peer in z_peers + [y_peer] + others:
+        pl.semaphore_signal(barrier, inc=1, device_id=peer, device_id_type=MESH)
+    pl.semaphore_wait(barrier, len(z_peers) + 1 + len(others))
+
+    users_copy = pltpu.make_async_remote_copy(
+        users_ref, prior, user_sem.at[0], user_sem.at[1],
+        device_id=(pack, jnp.minimum(hist + 1, last_hist)), device_id_type=MESH,
+    )
+
+    @pl.when(hist < last_hist)
+    def _():
+        users_copy.start()
+
+    my_rows = pl.ds(pl.multiple_of(hist * quarter, quarter), quarter)
+    x_rows = pl.ds(pl.multiple_of(((1 - x) * 2 + core) * quarter, quarter), quarter)
+    core_rows = pl.ds(pl.multiple_of(core * half, half), half)
+
+    started = []
+
+    def send(at, src, dst, peer):
+        copy = pltpu.make_async_remote_copy(
+            src, dst, send_sem.at[at], recv_sem.at[at], device_id=peer, device_id_type=MESH
+        )
+        copy.start()
+        started.append(copy)
+
+    def arrived(at, where):
+        pltpu.make_async_remote_copy(
+            where, where, send_sem.at[at], recv_sem.at[at], device_id=c_peer, device_id_type=MESH
+        ).wait_recv()
+
+    for d in (1, 3, 2):
+        send(Z_AT + d - 1, w_hbm.at[my_rows], w.at[pack, my_rows], z_peers[d - 1])
+    send(Y_AT, w_hbm.at[core_rows], w.at[pack, core_rows], y_peer)
+
+    def part(shard, rows):
+        return w.at[shard, rows]
+
+    def on_z(d):
+        here = part(pack_of(-d, 0), my_rows)
+        arrived(Z_AT + d - 1, here)
+        send(X_AT + (d - 1) * 2, here, here, x_peer)
+        send(Y_AT + d, here, here, y_peer)
+        send(C_AT + Z_AT + d - 1, here, here, c_peer)
+
+    def on_y(d):
+        here = part(pack_of(-d, 1), core_rows if d == 0 else my_rows)
+        arrived(Y_AT + d, here)
+        if d > 0:
+            send(X_AT + (d - 1) * 2 + 1, here, here, x_peer)
+        send(C_AT + Y_AT + d, here, here, c_peer)
+
+    def on_x(d, dy):
+        here = part(pack_of(-d, dy), x_rows)
+        at = X_AT + (d - 1) * 2 + dy
+        arrived(at, here)
+        send(C_AT + at, here, here, c_peer)
+
+    def wait_core(d, dy):
+        shard = pack_of(-d, dy)
+        if d == 0:
+            arrived(C_AT + Y_AT, part(shard, core_rows))
+        else:
+            arrived(C_AT + (Y_AT + d if dy else Z_AT + d - 1), part(shard, my_rows))
+            arrived(C_AT + X_AT + (d - 1) * 2 + dy, part(shard, x_rows))
+
+    square = (GROUP, GROUP)
+    row_at = lax.broadcasted_iota(jnp.int32, square, 0)
+    col_at = lax.broadcasted_iota(jnp.int32, square, 1)
+
+    def user_row(ref, c):
+        return ref[:, c * GROUP:(c + 1) * GROUP].astype(F32)
+
+    def last_of(ref, c):
+        return jnp.broadcast_to(user_row(ref, c)[:, GROUP - 1:], (1, GROUP))
+
+    for c in range(blocks):
+        across = jnp.broadcast_to(user_row(users_ref, c), square)
+        down = across.T
+        same[c] = jnp.where(jnp.logical_and(across == down, row_at >= col_at), 1.0, 0.0)
+        rows_last[c] = jnp.where(down == last_of(users_ref, c), 1.0, 0.0)
+        if c > 0:
+            opened[c] = jnp.where(down == last_of(users_ref, c - 1), 1.0, 0.0)
+
+    def log_decay(head):
+        return jnp.log1p(-jnp.full((1, HEAD_DIM), rate_ref[head], F32))
+
+    loads[0].wait()
+    loads[1].wait()
+
+    def states(head, carry):
+        cols = pl.ds(pl.multiple_of(head * HEAD_DIM, HEAD_DIM), HEAD_DIM)
+        decay = log_decay(head)
+        tail = jnp.exp((GROUP - 1 - row_at).astype(F32) * decay)
+        step = jnp.exp(GROUP * decay)
+        state = None
+        for c in range(blocks):
+            events = slice(c * GROUP, (c + 1) * GROUP)
+            scaled = (k[events, cols].astype(F32) * (tail * rows_last[c])).astype(BF16)
+            own = lax.dot_general(
+                scaled, v[events, cols], (((0,), (0,)), ((), ())), preferred_element_type=F32
+            )
+            if c == 0:
+                state = own
+            else:
+                keep = jnp.where(last_of(users_ref, c) == last_of(users_ref, c - 1), step, 0.0)
+                state = keep * state + own
+            if c + 1 < blocks:
+                local[head, c] = state
+            else:
+                final[head] = state
+        return carry
+
+    heads_part = HEADS // PARTS
+
+    lax.fori_loop(0, HEADS, states, 0)
+
+    @pl.when(hist > 0)
+    def _():
+        users_copy.wait_recv()
+
+    @pl.when(hist == 0)
+    def _():
+        prior[...] = jnp.full(prior.shape, -1, jnp.int32)
+        s_in[...] = jnp.zeros(s_in.shape, BF16)
+
+    before_all = last_of(prior, blocks - 1)
+    down = jnp.broadcast_to(user_row(users_ref, 0), square).T
+    opened[0] = jnp.where(down == before_all, 1.0, 0.0)
+
+    def state_copy(i):
+        heads = pl.ds(i * heads_part, heads_part)
+        return pltpu.make_async_remote_copy(
+            s_out.at[heads], s_in.at[heads], state_send.at[i], state_recv.at[i],
+            device_id=(pack, jnp.minimum(hist + 1, last_hist)), device_id_type=MESH,
+        )
+
+    def pass_on(i):
+        @pl.when(hist > 0)
+        def _():
+            state_copy(i).wait_recv()
+
+        @pl.when(hist < last_hist)
+        def _():
+            for head in range(i * heads_part, (i + 1) * heads_part):
+                whole = jnp.exp(length * log_decay(head))
+                keep = jnp.where(last_of(users_ref, blocks - 1) == before_all, whole, 0.0)
+                s_out[head] = (keep * s_in[head].astype(F32) + final[head]).astype(BF16)
+            state_copy(i).start()
+
+    pass_on(0)
+    on_z(1)
+    pass_on(1)
+    on_y(0)
+    on_z(3)
+    pass_on(2)
+    on_z(2)
+    pass_on(3)
+    loads[2].wait()
+    loads[3].wait()
+
+    def retain(head, carry):
+        cols = pl.ds(pl.multiple_of(head * HEAD_DIM, HEAD_DIM), HEAD_DIM)
+        decay = log_decay(head)
+        within = jnp.exp(jnp.maximum(row_at - col_at, 0).astype(F32) * decay)
+        reach = jnp.exp((row_at + 1).astype(F32) * decay)
+        gain = gain_ref[:, cols]
+        came = s_in[head].astype(F32)
+        for c in range(blocks):
+            events = slice(c * GROUP, (c + 1) * GROUP)
+            qb, vb = q[events, cols], v[events, cols]
+            scores = lax.dot_general(
+                qb, k[events, cols], (((1,), (1,)), ((), ())), preferred_element_type=F32
+            )
+            weights = (scores * (within * same[c])).astype(BF16)
+            if c == 0:
+                entering = s_in[head]
+            else:
+                keep = jnp.where(last_of(users_ref, c - 1) == before_all, jnp.exp(c * GROUP * decay), 0.0)
+                entering = (local[head, c - 1] + keep * came).astype(BF16)
+            reached = (qb.astype(F32) * (reach * opened[c])).astype(BF16)
+            kept = jnp.dot(
+                jnp.concatenate([weights, reached], axis=1),
+                jnp.concatenate([vb, entering], axis=0),
+                preferred_element_type=F32,
+            )
+            mean = jnp.mean(kept, axis=1, keepdims=True)
+            centred = kept - mean
+            variance = jnp.mean(centred * centred, axis=1, keepdims=True)
+            normed = centred * lax.rsqrt(variance + 1e-05) * gain
+            a = g[events, cols].astype(F32)
+            gated[events, cols] = (a / (1.0 + jnp.exp(-a)) * normed).astype(BF16)
+        return carry
+
+    events_after = {
+        0: [lambda: on_y(1)],
+        1: [lambda: on_y(3)],
+        2: [lambda: on_y(2)],
+        3: [lambda: on_x(1, 0)],
+        4: [lambda: on_x(3, 0)],
+        5: [lambda: on_x(1, 1)],
+        6: [lambda: on_x(3, 1)],
+        7: [],
+    }
+    for i in range(8):
+        lax.fori_loop(i * 2, i * 2 + 2, retain, 0)
+        for event in events_after[i]:
+            event()
+
+    tile = 512
+
+    def project(shards, first=False, last=False):
+        def body(j, carry):
+            cols = pl.ds(pl.multiple_of(j * tile, tile), tile)
+            total = None if first else acc[:, cols]
+            for shard in shards:
+                rows = pl.ds(pl.multiple_of(shard * depth, depth), depth)
+                term = jnp.dot(gated[:, rows], w[shard, :, cols], preferred_element_type=F32)
+                total = term if total is None else total + term
+            if last:
+                out[:, cols] = total.astype(BF16)
+            else:
+                acc[:, cols] = total
+            return carry
+
+        lax.fori_loop(0, width // tile, body, 0)
+
+    loads[4].wait()
+    wait_core(0, 1)
+    project([pack, pack_of(0, 1)], first=True)
+    on_x(2, 0)
+    wait_core(1, 0)
+    project([pack_of(-1, 0)])
+    wait_core(3, 0)
+    project([pack_of(-3, 0)])
+    wait_core(1, 1)
+    project([pack_of(-1, 1)])
+    on_x(2, 1)
+    wait_core(3, 1)
+    project([pack_of(-3, 1)])
+    wait_core(2, 0)
+    project([pack_of(-2, 0)])
+    wait_core(2, 1)
+    project([pack_of(-2, 1)], last=True)
+    store = pltpu.make_async_copy(out, o_hbm, load_sem.at[0])
+    store.start()
+    for copy in started:
+        copy.wait_send()
+
+    @pl.when(hist < last_hist)
+    def _():
+        users_copy.wait_send()
+        for i in range(PARTS):
+            state_copy(i).wait_send()
+
+    store.wait()
+
+
+def local_fused(queries, keys, values, gates, user_ids, forget_rate, norm_gain, w_out):
+    length, width = queries.shape[1:]
+    depth = w_out.shape[0]
+    blocks = length // GROUP
+    here = pl.BlockSpec(memory_space=pl.ANY)
+    vmem = pl.BlockSpec(memory_space=pltpu.VMEM)
+    big = pltpu.VMEM((length, width), BF16)
+    square = (HEAD_DIM, HEAD_DIM)
+    mixed = pl.pallas_call(
+        fused,
+        out_shape=jax.ShapeDtypeStruct((length, width), BF16),
+        in_specs=[pl.BlockSpec(memory_space=pltpu.SMEM), here, here, here, here, vmem, vmem, here],
+        out_specs=here,
+        scratch_shapes=[
+            big, big, big, big,
+            pltpu.VMEM((width // depth, depth, width), BF16),
+            big,
+            pltpu.VMEM((length, width), F32),
+            big,
+            pltpu.VMEM((HEADS, blocks - 1) + square, F32),
+            pltpu.VMEM((HEADS,) + square, F32),
+            pltpu.VMEM((HEADS,) + square, BF16),
+            pltpu.VMEM((HEADS,) + square, BF16),
+            pltpu.VMEM((1, length), jnp.int32),
+            pltpu.VMEM((blocks, GROUP, GROUP), F32),
+            pltpu.VMEM((blocks, GROUP, GROUP), F32),
+            pltpu.VMEM((blocks, GROUP, GROUP), F32),
+            pltpu.SemaphoreType.DMA((5,)),
+            pltpu.SemaphoreType.DMA((COPIES,)),
+            pltpu.SemaphoreType.DMA((COPIES,)),
+            pltpu.SemaphoreType.DMA((PARTS,)),
+            pltpu.SemaphoreType.DMA((PARTS,)),
+            pltpu.SemaphoreType.DMA((2,)),
+        ],
+        compiler_params=pltpu.CompilerParams(
+            collective_id=0, has_side_effects=True, vmem_limit_bytes=56 * 1024 * 1024
+        ),
+        cost_estimate=pl.CostEstimate(
+            flops=2 * length * width * (width + 4 * HEAD_DIM), bytes_accessed=12 * length * width, transcendentals=0
+        ),
+    )(
+        forget_rate, queries[0], keys[0], values[0], gates[0], user_ids, norm_gain.reshape(1, width), w_out,
+    )
+    return mixed[None]
+
+
 def solution(mesh):
     in_specs = (
         P("pack", "hist", None),
@@ -114,4 +466,5 @@
         P("pack", None),
     )
     out_specs = P("pack", "hist", None)
+    local = local_fused if fits(mesh) else local_any
     return jax.shard_map(local, mesh=mesh, in_specs=in_specs, out_specs=out_specs, check_vma=False)

time: 228 us -> 78.6 us (0.34)
  the two profiles are of different devices: /device:TPU:0 before, /device:TPU:17 now
where the time goes in v1:
time: 78.6 us; the launch traced here: 78.4 us
  Pallas kernels  75.2 us (96%)
  local copies, waits for them, and re-layouts  3.16 us (4%)
    pallas_call x1, Pallas kernels, local_fused(): pl.pallas_call(fused, out_shape=jax.ShapeDtypeStruct((length, width), BF1...  75.2 us
    unnamed x1, local copies, waits for them, and re-layouts  3.16 us

profile of v1, /device:TPU:17, one launch (start us, length us, event | category | flops | bytes accessed | tf_op | source)
XLA Modules:
  0.0 78.4 jit_solution(15916680469573482968)
XLA Ops:
  0.0 75.2 %shard_map.82 = bf16[512,2048]{1,0:T(8,128)(2,1)} custom-call(f32[16]{0:T(128)} %rate_ref.1, bf16[512,2048]{1,0:T(8,128)(2,1)} %bitcast.7, bf16[512,2048]{1,0:T(8,128)(2,1)} %bitcast.8, bf16[512,2048]{1,0:T(8,128)(2,1)} %bitcast.9, bf16[512,2048]{1,0:T(8,128)(2,1)} %bitcast.10, s32[1,512]{1,0:T(1,128)} %users_ref.1, f32[1,2048]{1,0:T(1,128)} %bitcast.11, ...), custom_call_target="tpu_custom_call" | custom-call | flops 5368709120 | bytes 12582912 | tf_op jit(solution)/shard_map/pallas_call | solution.py:419
  75.2 3.2 %copy.10 = bf16[1,512,2048]{2,1,0:T(8,128)(2,1)} copy(bf16[1,512,2048]{2,1,0:T(8,128)(2,1)} %bitcast.6) | data formatting | bytes 4194304

commit v2 on v1

--- a/solution.py
+++ b/solution.py
@@ -114,7 +114,8 @@
 F32 = jnp.float32
 BF16 = jnp.bfloat16
 PARTS = 4
-Z_AT, Y_AT, X_AT, C_AT, COPIES = 0, 3, 7, 13, 26
+A_AT, B_AT, Y0_AT, YA_AT, X1_AT, X2_AT = 0, 4, 8, 10, 13, 16
+A_IN, B_IN, CORE, SPARE, COPIES = 0, 4, 20, 40, 56
 
 
 def fits(mesh):
@@ -163,58 +164,105 @@
     def _():
         users_copy.start()
 
-    my_rows = pl.ds(pl.multiple_of(hist * quarter, quarter), quarter)
-    x_rows = pl.ds(pl.multiple_of(((1 - x) * 2 + core) * quarter, quarter), quarter)
-    core_rows = pl.ds(pl.multiple_of(core * half, half), half)
+    unit = depth // 8
+    base = core * half
+
+    def rows_at(first, count):
+        return pl.ds(pl.multiple_of(base + first * unit, unit), count * unit)
+
+    z_rows, z_more, x_own = rows_at(2 * x, 2), rows_at(2 - x, 1), rows_at(3 * x, 1)
+    x_in, x_in_own = rows_at(2 - 2 * x, 2), rows_at(3 - 3 * x, 1)
+    y_rows = [rows_at(0, 2), rows_at(2, 2)]
+    first = jnp.where(z == 0, 1, z - 1)
+    third = jnp.where(z < 2, 3, 0)
+    sources = [first, 6 - z - first - third, third]
 
     started = []
 
-    def send(at, src, dst, peer):
-        copy = pltpu.make_async_remote_copy(
-            src, dst, send_sem.at[at], recv_sem.at[at], device_id=peer, device_id_type=MESH
+    def copy_of(at_send, at, where, peer, src=None):
+        return pltpu.make_async_remote_copy(
+            where if src is None else src, where, send_sem.at[at_send], recv_sem.at[at],
+            device_id=peer, device_id_type=MESH,
         )
-        copy.start()
-        started.append(copy)
+
+    def send(at, where, peer, src=None, when=None, at_send=None):
+        copy = copy_of(at if at_send is None else at_send, at, where, peer, src)
+        if when is None:
+            copy.start()
+        else:
+            pl.when(when)(copy.start)
+        started.append((copy, when))
 
     def arrived(at, where):
-        pltpu.make_async_remote_copy(
-            where, where, send_sem.at[at], recv_sem.at[at], device_id=c_peer, device_id_type=MESH
-        ).wait_recv()
-
-    for d in (1, 3, 2):
-        send(Z_AT + d - 1, w_hbm.at[my_rows], w.at[pack, my_rows], z_peers[d - 1])
-    send(Y_AT, w_hbm.at[core_rows], w.at[pack, core_rows], y_peer)
-
-    def part(shard, rows):
-        return w.at[shard, rows]
-
-    def on_z(d):
-        here = part(pack_of(-d, 0), my_rows)
-        arrived(Z_AT + d - 1, here)
-        send(X_AT + (d - 1) * 2, here, here, x_peer)
-        send(Y_AT + d, here, here, y_peer)
-        send(C_AT + Z_AT + d - 1, here, here, c_peer)
-
-    def on_y(d):
-        here = part(pack_of(-d, 1), core_rows if d == 0 else my_rows)
-        arrived(Y_AT + d, here)
-        if d > 0:
-            send(X_AT + (d - 1) * 2 + 1, here, here, x_peer)
-        send(C_AT + Y_AT + d, here, here, c_peer)
-
-    def on_x(d, dy):
-        here = part(pack_of(-d, dy), x_rows)
-        at = X_AT + (d - 1) * 2 + dy
-        arrived(at, here)
-        send(C_AT + at, here, here, c_peer)
-
-    def wait_core(d, dy):
-        shard = pack_of(-d, dy)
-        if d == 0:
-            arrived(C_AT + Y_AT, part(shard, core_rows))
-        else:
-            arrived(C_AT + (Y_AT + d if dy else Z_AT + d - 1), part(shard, my_rows))
-            arrived(C_AT + X_AT + (d - 1) * 2 + dy, part(shard, x_rows))
+        copy_of(0, at, where, c_peer).wait_recv()
+
+    def part(z_from, dy, rows):
+        return w.at[z_from * 2 + (y if dy == 0 else 1 - y), rows]
+
+    z_up = (jnp.minimum(z + 1, 3) * 2 + y, hist)
+    z_down = (jnp.maximum(z - 1, 0) * 2 + y, hist)
+
+    def send_z(kind, rows):
+        src, where = w_hbm.at[rows], w.at[pack, rows]
+        send(kind + z, where, z_up, src, z < 3, SPARE + kind)
+        send(kind + z, where, z_down, src, z > 0, SPARE + kind + 1)
+
+    def send_y0(i):
+        send(Y0_AT + i, w.at[pack, y_rows[i]], y_peer, w_hbm.at[y_rows[i]])
+
+    def pass_z(kind, o, here):
+        z_from = sources[o]
+        at_send = SPARE + 8 + kind + o
+        send(kind + z_from, here, z_up, None, jnp.logical_and(z_from < z, z < 3), at_send)
+        send(kind + z_from, here, z_down, None, jnp.logical_and(z_from > z, z > 0), at_send)
+
+    def on_a(o):
+        here = part(sources[o], 0, z_rows)
+        arrived(A_AT + sources[o], here)
+        pass_z(A_AT, o, here)
+        send(YA_AT + o, here, y_peer)
+        send(X1_AT + o, part(sources[o], 0, x_own), x_peer)
+        send(CORE + A_IN + o, here, c_peer)
+
+    def on_b(o):
+        here = part(sources[o], 0, z_more)
+        arrived(B_AT + sources[o], here)
+        pass_z(B_AT, o, here)
+        send(CORE + B_IN + o, here, c_peer)
+
+    def on_y0(i):
+        here = part(z, 1, y_rows[i])
+        arrived(Y0_AT + i, here)
+        send(CORE + Y0_AT + i, here, c_peer)
+
+    def on_ya(o):
+        here = part(sources[o], 1, z_rows)
+        arrived(YA_AT + o, here)
+        send(X2_AT + o, here, x_peer)
+        send(CORE + YA_AT + o, here, c_peer)
+
+    def on_x1(o):
+        here = part(sources[o], 0, x_in_own)
+        arrived(X1_AT + o, here)
+        send(CORE + X1_AT + o, here, c_peer)
+
+    def on_x2(o):
+        here = part(sources[o], 1, x_in)
+        arrived(X2_AT + o, here)
+        send(CORE + X2_AT + o, here, c_peer)
+
+    def wait_core(o):
+        if o is None:
+            for i in range(2):
+                arrived(CORE + Y0_AT + i, part(z, 1, y_rows[i]))
+            return
+        for kind, dy, rows in [
+            (A_IN, 0, z_rows), (B_IN, 0, z_more), (X1_AT, 0, x_in_own), (YA_AT, 1, z_rows), (X2_AT, 1, x_in)
+        ]:
+            arrived(CORE + kind + o, part(sources[o], dy, rows))
+
+    send_z(A_AT, z_rows)
+    send_y0(0)
 
     square = (GROUP, GROUP)
     row_at = lax.broadcasted_iota(jnp.int32, square, 0)
@@ -265,21 +313,6 @@
 
     heads_part = HEADS // PARTS
 
-    lax.fori_loop(0, HEADS, states, 0)
-
-    @pl.when(hist > 0)
-    def _():
-        users_copy.wait_recv()
-
-    @pl.when(hist == 0)
-    def _():
-        prior[...] = jnp.full(prior.shape, -1, jnp.int32)
-        s_in[...] = jnp.zeros(s_in.shape, BF16)
-
-    before_all = last_of(prior, blocks - 1)
-    down = jnp.broadcast_to(user_row(users_ref, 0), square).T
-    opened[0] = jnp.where(down == before_all, 1.0, 0.0)
-
     def state_copy(i):
         heads = pl.ds(i * heads_part, heads_part)
         return pltpu.make_async_remote_copy(
@@ -287,27 +320,46 @@
             device_id=(pack, jnp.minimum(hist + 1, last_hist)), device_id_type=MESH,
         )
 
-    def pass_on(i):
-        @pl.when(hist > 0)
+    @pl.when(hist == 0)
+    def _():
+        prior[...] = jnp.full(prior.shape, -1, jnp.int32)
+        s_in[...] = jnp.zeros(s_in.shape, BF16)
+
+    for i in range(PARTS):
+        lax.fori_loop(i * heads_part, (i + 1) * heads_part, states, 0)
+
+        @pl.when(hist == 0)
+        def _():
+            heads = slice(i * heads_part, (i + 1) * heads_part)
+            s_out[heads] = final[heads].astype(BF16)
+            state_copy(i).start()
+
+    @pl.when(hist > 0)
+    def _():
+        users_copy.wait_recv()
+
+    before_all = last_of(prior, blocks - 1)
+    down = jnp.broadcast_to(user_row(users_ref, 0), square).T
+    opened[0] = jnp.where(down == before_all, 1.0, 0.0)
+
+    def pass_on(i, at_hist):
+        @pl.when(hist == at_hist)
         def _():
             state_copy(i).wait_recv()
-
-        @pl.when(hist < last_hist)
-        def _():
-            for head in range(i * heads_part, (i + 1) * heads_part):
-                whole = jnp.exp(length * log_decay(head))
-                keep = jnp.where(last_of(users_ref, blocks - 1) == before_all, whole, 0.0)
-                s_out[head] = (keep * s_in[head].astype(F32) + final[head]).astype(BF16)
-            state_copy(i).start()
-
-    pass_on(0)
-    on_z(1)
-    pass_on(1)
-    on_y(0)
-    on_z(3)
-    pass_on(2)
-    on_z(2)
-    pass_on(3)
+            if at_hist < last_hist:
+                for head in range(i * heads_part, (i + 1) * heads_part):
+                    whole = jnp.exp(length * log_decay(head))
+                    keep = jnp.where(last_of(users_ref, blocks - 1) == before_all, whole, 0.0)
+                    s_out[head] = (keep * s_in[head].astype(F32) + final[head]).astype(BF16)
+                state_copy(i).start()
+
+    for i in range(PARTS):
+        pass_on(i, 1)
+    on_a(0)
+    send_y0(1)
+    pass_on(0, 2)
+    pass_on(1, 2)
+    pass_on(0, 3)
     loads[2].wait()
     loads[3].wait()
 
@@ -344,20 +396,23 @@
             gated[events, cols] = (a / (1.0 + jnp.exp(-a)) * normed).astype(BF16)
         return carry
 
-    events_after = {
-        0: [lambda: on_y(1)],
-        1: [lambda: on_y(3)],
-        2: [lambda: on_y(2)],
-        3: [lambda: on_x(1, 0)],
-        4: [lambda: on_x(3, 0)],
-        5: [lambda: on_x(1, 1)],
-        6: [lambda: on_x(3, 1)],
-        7: [],
-    }
-    for i in range(8):
+    def send_more():
+        send_z(B_AT, z_more)
+
+    events_after = [
+        [(on_y0, 0), (pass_on, 2, 2), (pass_on, 3, 2)],
+        [(on_a, 1), (on_ya, 0), (send_more,), (pass_on, 1, 3)],
+        [(on_x1, 0), (on_a, 2)],
+        [(on_ya, 1), (on_y0, 1), (pass_on, 2, 3)],
+        [(on_b, 0), (on_x2, 0)],
+        [(on_ya, 2), (on_x1, 1), (pass_on, 3, 3)],
+        [(on_b, 1), (on_x2, 1)],
+        [(on_x1, 2)],
+    ]
+    for i, events in enumerate(events_after):
         lax.fori_loop(i * 2, i * 2 + 2, retain, 0)
-        for event in events_after[i]:
-            event()
+        for event, *which in events:
+            event(*which)
 
     tile = 512
 
@@ -377,27 +432,27 @@
 
         lax.fori_loop(0, width // tile, body, 0)
 
+    def pair(z_from):
+        return [z_from * 2 + y, z_from * 2 + 1 - y]
+
     loads[4].wait()
-    wait_core(0, 1)
-    project([pack, pack_of(0, 1)], first=True)
-    on_x(2, 0)
-    wait_core(1, 0)
-    project([pack_of(-1, 0)])
-    wait_core(3, 0)
-    project([pack_of(-3, 0)])
-    wait_core(1, 1)
-    project([pack_of(-1, 1)])
-    on_x(2, 1)
-    wait_core(3, 1)
-    project([pack_of(-3, 1)])
-    wait_core(2, 0)
-    project([pack_of(-2, 0)])
-    wait_core(2, 1)
-    project([pack_of(-2, 1)], last=True)
+    wait_core(None)
+    project(pair(z), first=True)
+    on_b(2)
+    wait_core(0)
+    project(pair(sources[0]))
+    on_x2(2)
+    wait_core(1)
+    project(pair(sources[1]))
+    wait_core(2)
+    project(pair(sources[2]), last=True)
     store = pltpu.make_async_copy(out, o_hbm, load_sem.at[0])
     store.start()
-    for copy in started:
-        copy.wait_send()
+    for copy, when in started:
+        if when is None:
+            copy.wait_send()
+        else:
+            pl.when(when)(copy.wait_send)
 
     @pl.when(hist < last_hist)
     def _():

time: 78.6 us -> 60.7 us (0.77)
  the two profiles are of different devices: /device:TPU:17 before, /device:TPU:0 now
where the time goes in v2:
time: 60.7 us; the launch traced here: 60.5 us
  Pallas kernels  57.3 us (94%)
  local copies, waits for them, and re-layouts  3.16 us (5%)
    pallas_call x1, Pallas kernels, local_fused(): pl.pallas_call(fused, out_shape=jax.ShapeDtypeStruct((length, width), BF1...  57.3 us
    unnamed x1, local copies, waits for them, and re-layouts  3.16 us

profile of v2, /device:TPU:0, one launch (start us, length us, event | category | flops | bytes accessed | tf_op | source)
XLA Modules:
  0.0 60.5 jit_solution(826087964502872116)
XLA Ops:
  0.0 57.3 %shard_map.82 = bf16[512,2048]{1,0:T(8,128)(2,1)} custom-call(f32[16]{0:T(128)} %rate_ref.1, bf16[512,2048]{1,0:T(8,128)(2,1)} %bitcast.7, bf16[512,2048]{1,0:T(8,128)(2,1)} %bitcast.8, bf16[512,2048]{1,0:T(8,128)(2,1)} %bitcast.9, bf16[512,2048]{1,0:T(8,128)(2,1)} %bitcast.10, s32[1,512]{1,0:T(1,128)} %users_ref.1, f32[1,2048]{1,0:T(1,128)} %bitcast.11, ...), custom_call_target="tpu_custom_call" | custom-call | flops 5368709120 | bytes 12582912 | tf_op jit(solution)/shard_map/pallas_call | solution.py:474
  57.3 3.2 %copy.10 = bf16[1,512,2048]{2,1,0:T(8,128)(2,1)} copy(bf16[1,512,2048]{2,1,0:T(8,128)(2,1)} %bitcast.6) | data formatting | bytes 4194304
